TPU v7x, 32 devices: a whole 2x2x4 slice. The times are simulated.
32 devices in a mesh: dp: 16 (over z, x, core), tensor: 2 (over y).
Axes of the slice: x: 2, y: 2, z: 4, core: 2. Of those that a mesh axis runs over, the one named last changes fastest.
Arguments:
- grad_out: bfloat16 [8192, 8192], P(('dp', 'tensor')), may hold values from -60 to 60
- out_weight: bfloat16 [8192, 8192], P('tensor', 'dp'), may hold values from -0.0625 to 0.0625
- queries: bfloat16 [8192, 8192], P('dp', 'tensor'), may hold values from -150 to 150, as said below
- keys: bfloat16 [8192, 1024], P('dp', 'tensor'), may hold values from -7 to 7, as said below
- values: bfloat16 [8192, 1024], P('dp', 'tensor'), may hold values from -6 to 6
- prefix_keys: bfloat16 [128, 1024], P(None, 'tensor'), may hold values from -6 to 6
- prefix_values: bfloat16 [128, 1024], P(None, 'tensor'), may hold values from -6 to 6
Outputs:
- grad_queries: bfloat16 [8192, 8192], P('dp', 'tensor')
- grad_keys: bfloat16 [8192, 1024], P('dp', 'tensor')
- grad_values: bfloat16 [8192, 1024], P('dp', 'tensor')
- grad_prefix_keys: float32 [128, 1024], P(None, 'tensor')
- grad_prefix_values: float32 [128, 1024], P(None, 'tensor')
Inputs may be any that keep to these rules, and one draw needn't show every extreme that they name: `keys`: keys of order one. `queries`: queries of order one in most rows.
All inputs are finite; a program needn't handle non-finite values.
Results may differ from a plain program's by a relative error of at most 0.015.
Values may be sent and summed in bfloat16 or wider, within the bound.
A program may use at most 320 MiB of HBM per device.

v0:
```python
import jax
import jax.numpy as jnp
from jax import lax
from jax.sharding import PartitionSpec as P

QH = 64
KVH = 8
HD = 128
PREFIX = 128


def reduce_prefix(key_part, value_part):
    return (
        lax.psum(key_part.astype(jnp.bfloat16), "dp").astype(jnp.float32),
        lax.psum(value_part.astype(jnp.bfloat16), "dp").astype(jnp.float32),
    )


def shards(grad_out, out_weight, queries, keys, values, prefix_keys, prefix_values):
    full_rows = lax.all_gather(grad_out, "tensor", axis=0, tiled=True)
    length = full_rows.shape[0]
    d_attn = lax.dot_general(
        full_rows,
        lax.all_gather(out_weight, "dp", axis=1, tiled=True),
        (((1,), (1,)), ((), ())),
        preferred_element_type=jnp.float32,
    ).astype(jnp.bfloat16)
    scale = HD ** (-0.5)
    kv_local = keys.shape[1] // HD
    group = QH // KVH
    query_wide = queries.reshape(length, kv_local, group, HD)
    dattn_wide = d_attn.reshape(length, kv_local, group, HD)
    key_all = jnp.concatenate(
        [prefix_keys.reshape(PREFIX, kv_local, HD), keys.reshape(length, kv_local, HD)], 0
    )
    value_all = jnp.concatenate(
        [prefix_values.reshape(PREFIX, kv_local, HD), values.reshape(length, kv_local, HD)], 0
    )
    scores = (
        jnp.einsum("ichd,jcd->chij", query_wide, key_all, preferred_element_type=jnp.float32)
        * scale
    )
    row_ids = jnp.arange(length, dtype=jnp.int32)[:, None]
    col_ids = jnp.arange(PREFIX + length, dtype=jnp.int32)[None, :]
    visible = (col_ids < PREFIX) | (col_ids - PREFIX <= row_ids)
    scores = jnp.where(visible, scores, -jnp.inf)
    top = jnp.max(scores, axis=-1, keepdims=True)
    expo = jnp.exp(scores - top)
    probs = expo / jnp.sum(expo, axis=-1, keepdims=True)
    grad_probs = jnp.einsum(
        "ichd,jcd->chij", dattn_wide, value_all, preferred_element_type=jnp.float32
    )
    row_dot = jnp.sum(probs * grad_probs, axis=-1, keepdims=True)
    grad_scores = probs * (grad_probs - row_dot)
    probs_low = probs.astype(jnp.bfloat16)
    grad_low = grad_scores.astype(jnp.bfloat16)
    key_grad = (
        jnp.einsum("chij,ichd->jcd", grad_low, query_wide, preferred_element_type=jnp.float32)
        * scale
    )
    value_grad = jnp.einsum(
        "chij,ichd->jcd", probs_low, dattn_wide, preferred_element_type=jnp.float32
    )
    summed_k, summed_v = reduce_prefix(
        key_grad[:PREFIX].reshape(PREFIX, kv_local * HD),
        value_grad[:PREFIX].reshape(PREFIX, kv_local * HD),
    )
    token_kgrad = key_grad[PREFIX:]
    token_vgrad = value_grad[PREFIX:]
    grad_query = (
        jnp.einsum("chij,jcd->ichd", grad_low, key_all, preferred_element_type=jnp.float32) * scale
    )
    return (
        grad_query.reshape(length, kv_local * group * HD).astype(jnp.bfloat16),
        token_kgrad.reshape(length, kv_local * HD).astype(jnp.bfloat16),
        token_vgrad.reshape(length, kv_local * HD).astype(jnp.bfloat16),
        summed_k,
        summed_v,
    )


def solution(mesh):
    in_specs = (
        P(("dp", "tensor"), None),
        P("tensor", "dp"),
        P("dp", "tensor"),
        P("dp", "tensor"),
        P("dp", "tensor"),
        P(None, "tensor"),
        P(None, "tensor"),
    )
    out_specs = (
        P("dp", "tensor"),
        P("dp", "tensor"),
        P("dp", "tensor"),
        P(None, "tensor"),
        P(None, "tensor"),
    )
    return jax.shard_map(shards, mesh=mesh, in_specs=in_specs, out_specs=out_specs, check_vma=False)
```

profile of v0, /device:TPU:0, one launch (start us, length us, event | category | flops | bytes accessed | tf_op | source)
XLA Modules:
  0.0 715.9 jit_solution(15269781383410972993)
XLA Ops:
  7.2 0.0 copy-start.8
  7.2 0.0 copy-start.9
  7.2 0.0 copy-start.6
  7.2 0.0 copy-start.7
  7.2 0.0 all-gather.3.cloned.1.call-start
  7.3 0.7 all-gather.3.cloned.1.call-update
  7.9 0.0 all-gather.5.cloned.1.call-start
  8.0 0.7 all-gather.5.cloned.1.call-update
  8.7 0.0 all-reduce.3.cloned.1.call-start
  8.7 0.0 copy-done.8
  8.7 0.1 copy.25
  8.9 0.1 copy.27
  9.0 0.0 copy-done.9
  9.0 0.0 copy-start.4
  9.0 0.1 copy.30
  9.2 0.1 copy.32
  9.3 0.0 copy-done.6
  9.3 0.2 copy.26
  9.5 0.3 copy.28
  9.8 0.0 copy-done.7
  9.8 0.0 copy-start.2
  9.8 0.2 copy.31
  10.0 0.3 copy.33
  10.3 6.4 copy.57
  16.7 0.3 fusion.16
  17.0 21.9 %fusion.31 = (f32[4,8,512]{2,1,0:T(8,128)S(1)}, f32[4,8,512,640]{2,3,1,0:T(8,128)}) fusion(pred[512,640]{0,1:T(8,128)(4,1)S(1)} %fusion.16, bf16[512,4,8,128]{0,3,2,1:T(8,128)(2,1)} %bitcast.89, bf16[512,4,128]{2,0,1:T(8,128)(2,1)S(1)} %copy.28, bf16[128,4,128]{2,0,1:T(8,128)(2,1)S(1)} %copy.27), kind=kOutput, calls=%fused_computation.42 | convolution fusion | flops 2727608832 | bytes 47185920 | tf_op jit(solution)/shard_map/sub | solution.py:48
  39.0 0.0 copy-done.4
  39.0 0.0 copy-done.2
  39.0 77.4 %all-gather.3.cloned.1.call-done = bf16[512,8192]{1,0:T(8,128)(2,1)} async-done(((bf16[256,8192]{1,0:T(8,128)(2,1)}), bf16[512,8192]{1,0:T(8,128)(2,1)}) %all-gather.3.cloned.1.call-update) | async-done | bytes 8388624 | tf_op jit(solution)/shard_map/all_gather | solution.py:20
  116.3 327.7 %all-gather.5.cloned.1.call-done = bf16[4096,8192]{1,0:T(8,128)(2,1)} async-done(((bf16[4096,512]{1,0:T(8,128)(2,1)}), bf16[4096,8192]{1,0:T(8,128)(2,1)}) %all-gather.5.cloned.1.call-update) | async-done | bytes 67108880 | tf_op jit(solution)/shard_map/all_gather | solution.py:24
  444.0 42.9 %fusion.12 = bf16[64,8,32,128]{3,1,2,0:T(8,128)(2,1)} fusion(bf16[512,8192]{1,0:T(8,128)(2,1)} %all-gather.3.cloned.1.call-done, bf16[4096,8192]{1,0:T(8,128)(2,1)} %all-gather.5.cloned.1.call-done), kind=kOutput, calls=%fused_computation.18 | convolution fusion | flops 34361835520 | bytes 79691776 | tf_op jit(solution)/shard_map/dot_general | solution.py:22
  486.9 3.4 copy.58
  490.3 0.0 copy-start.1
  490.3 28.3 %fusion.1 = (f32[4,8,512]{2,1,0:T(8,128)S(1)}, f32[4,640,512,8]{2,1,3,0:T(8,128)}) fusion(f32[4,8,512,640]{2,3,1,0:T(8,128)} %get-tuple-element.20, f32[4,8,512]{2,1,0:T(8,128)S(1)} %get-tuple-element.19, bf16[512,4,8,128]{3,2,1,0:T(8,128)(2,1)S(1)} %bitcast.91, bf16[512,4,128]{2,0,1:T(8,128)(2,1)S(1)} %copy.33, bf16[128,4,128]{2,0,1:T(8,128)(2,1)S(1)} %copy.32), kind=kOutput, calls=%fused_computation.3 | convolution fusion | flops 2717106176 | bytes 88866816 | tf_op jit(solution)/shard_map/ichd,jcd->chij/dot_general | solution.py:50
  518.6 41.7 %fusion.30 = (bf16[4,8,512,640]{2,3,1,0:T(8,128)(2,1)}, bf16[4,8,512,640]{2,3,1,0:T(8,128)(2,1)}) fusion(f32[4,8,512,640]{2,3,1,0:T(8,128)} %get-tuple-element.20, f32[4,8,512]{2,1,0:T(8,128)S(1)} %get-tuple-element.19, f32[4,8,512]{2,1,0:T(8,128)S(1)} %get-tuple-element.21, f32[4,640,512,8]{2,1,3,0:T(8,128)} %get-tuple-element.22), kind=kLoop, calls=%fused_computation.41 | loop fusion | flops 52428800 | bytes 125960192 | tf_op jit(solution)/shard_map/convert_element_type | solution.py:55
  560.2 10.6 %fusion.18 = bf16[640,4,128]{0,2,1:T(8,128)(2,1)S(1)} fusion(bf16[4,8,512,640]{2,3,1,0:T(8,128)(2,1)} %get-tuple-element.18, bf16[512,4,8,128]{0,3,2,1:T(8,128)(2,1)S(1)} %bitcast.90), kind=kOutput, calls=%fused_computation.27 | convolution fusion | flops 2685009920 | bytes 25821184 | tf_op jit(solution)/shard_map/chij,ichd->jcd/dot_general | solution.py:58
  570.9 34.3 %copy.53 = bf16[4,8,512,640]{3,1,0,2:T(8,128)(2,1)} copy(bf16[4,8,512,640]{2,3,1,0:T(8,128)(2,1)} %get-tuple-element.17) | data formatting | bytes 41943040 | tf_op jit(solution)/shard_map/convert_element_type | solution.py:55
  605.2 10.2 %fusion.17 = bf16[640,4,128]{0,2,1:T(8,128)(2,1)S(1)} fusion(bf16[512,4,8,128]{3,2,1,0:T(8,128)(2,1)} %bitcast.92, bf16[4,8,512,640]{3,1,0,2:T(8,128)(2,1)} %copy.53), kind=kOutput, calls=%fused_computation.26 | convolution fusion | flops 2684682240 | bytes 25821184 | tf_op jit(solution)/shard_map/chij,ichd->jcd/dot_general | solution.py:61
  615.4 0.8 copy.42
  616.2 0.8 copy.41
  617.0 0.0 all-reduce.3.cloned.1.call-update
  617.0 12.5 %multiply_convert_fusion = bf16[4,128,8,512]{3,1,2,0:T(8,128)(2,1)} fusion(bf16[4,8,512,640]{2,3,1,0:T(8,128)(2,1)} %get-tuple-element.18, bf16[512,4,128]{2,0,1:T(8,128)(2,1)S(1)} %copy-done.3, bf16[128,4,128]{2,0,1:T(8,128)(2,1)S(1)} %copy-done.5), kind=kOutput, calls=%fused_computation.13 | convolution fusion | flops 2689859584 | bytes 25821184 | tf_op jit(solution)/shard_map/chij,jcd->ichd/dot_general | solution.py:71
  629.6 1.0 copy.45
  630.6 1.0 copy.44
  631.6 6.3 copy.43
  637.9 68.2 %all-reduce.3.cloned.1.call-done = (bf16[128,512]{1,0:T(8,128)(2,1)}, bf16[128,512]{1,0:T(8,128)(2,1)}) async-done(((bf16[128,512]{1,0:T(8,128)(2,1)}, bf16[128,512]{1,0:T(8,128)(2,1)}), (bf16[128,512]{1,0:T(8,128)(2,1)}, bf16[128,512]{1,0:T(8,128)(2,1)})) %all-reduce.3.cloned.1.call-update) | async-done | bytes 262160 | tf_op jit(solution)/shard_map/psum | solution.py:14
  706.1 1.6 convert_element_type.49
  707.8 1.6 convert_element_type.51
  (13 shorter events, 0.1 us)
Async XLA Ops:
  7.2 1.6 copy-start.8
  7.2 1.8 copy-start.9
  7.2 2.1 copy-start.6
  7.2 2.6 copy-start.7
  7.2 109.1 %all-gather.3.cloned.1.call-start = ((), (), s32[]{:S(2)}) async-start(), calls=%async_computation | async-start | bytes 12582912 | tf_op jit(solution)/shard_map/all_gather | solution.py:20
  7.9 436.1 %all-gather.5.cloned.1.call-start = ((), (), s32[]{:S(2)}) async-start(), calls=%async_computation.1 | async-start | bytes 71303168 | tf_op jit(solution)/shard_map/all_gather | solution.py:24
  8.7 697.4 %all-reduce.3.cloned.1.call-start = ((), (), s32[]{:S(2)}) async-start(), calls=%async_computation.2 | async-start | bytes 524288 | tf_op jit(solution)/shard_map/psum | solution.py:14
  9.0 29.9 %copy-start.4 = (bf16[128,4,128]{2,0,1:T(8,128)(2,1)}, bf16[128,4,128]{2,0,1:T(8,128)(2,1)S(1)}, u32[]{:S(2)}) copy-start(bf16[128,4,128]{2,0,1:T(8,128)(2,1)S(1)} %copy.27) | copy-start | bytes 393220
  9.8 29.2 %copy-start.2 = (bf16[512,4,128]{2,0,1:T(8,128)(2,1)}, bf16[512,4,128]{2,0,1:T(8,128)(2,1)S(1)}, u32[]{:S(2)}) copy-start(bf16[512,4,128]{2,0,1:T(8,128)(2,1)S(1)} %copy.28) | copy-start | bytes 1572868
  490.3 28.3 %copy-start.1 = (bf16[64,8,32,128]{3,2,1,0:T(8,128)(2,1)}, bf16[64,8,32,128]{3,2,1,0:T(8,128)(2,1)S(1)}, u32[]{:S(2)}) copy-start(bf16[64,8,32,128]{3,2,1,0:T(8,128)(2,1)S(1)} %copy.58) | copy-start | bytes 12582916
  518.6 41.7 %copy-start = (bf16[512,4096]{0,1:T(8,128)(2,1)S(1)}, bf16[512,4096]{0,1:T(8,128)(2,1)}, u32[]{:S(2)}) copy-start(bf16[512,4096]{0,1:T(8,128)(2,1)} %copy.57) | copy-start | bytes 12582916
  605.2 11.9 %copy-start.3 = (bf16[512,4,128]{2,0,1:T(8,128)(2,1)S(1)}, bf16[512,4,128]{2,0,1:T(8,128)(2,1)}, u32[]{:S(2)}) copy-start(bf16[512,4,128]{2,0,1:T(8,128)(2,1)} %copy-done.2) | copy-start | bytes 1572868
  605.2 11.9 %copy-start.5 = (bf16[128,4,128]{2,0,1:T(8,128)(2,1)S(1)}, bf16[128,4,128]{2,0,1:T(8,128)(2,1)}, u32[]{:S(2)}) copy-start(bf16[128,4,128]{2,0,1:T(8,128)(2,1)} %copy-done.4) | copy-start | bytes 393220
Sparse Core Ops, SparseCore 0:
  9.6 106.6 all-gather.2
  117.9 326.1 all-gather.4
  617.2 88.9 all-reduce.2
where the time goes:
time: 717 us; the launch traced here: 716 us
  waiting for transfers between devices  475 us (66%)
  matrix products  126 us (18%)
  local copies, waits for them, and re-layouts  55.6 us (8%)
  other arithmetic  45.2 us (6%)
  between operations  14 us (2%)
    all_gather x1, waiting for transfers between devices, shards(): lax.all_gather(out_weight, 'dp', axis=1, tiled=True)  328 us
    all_gather x1, waiting for transfers between devices, shards(): full_rows = lax.all_gather(grad_out, 'tensor', axis=0, tiled=True)  77.4 us
    psum x1, waiting for transfers between devices, reduce_prefix(): lax.psum(key_part.astype(jnp.bfloat16), 'dp').astype(jnp.float32)  68.2 us
    dot_general x1, matrix products, shards(): lax.dot_general(full_rows, lax.all_gather(out_weight, 'dp', axis=1, tiled...  42.9 us
    convert_element_type x1, other arithmetic, shards(): probs_low = probs.astype(jnp.bfloat16)  41.7 us
    convert_element_type x1, local copies, waits for them, and re-layouts, shards(): probs_low = probs.astype(jnp.bfloat16)  34.3 us
    dot_general x1, matrix products, shards(): jnp.einsum('ichd,jcd->chij', dattn_wide, value_all, preferred_element_typ...  28.3 us
    sub x1, matrix products, shards(): expo = jnp.exp(scores - top)  21.9 us
  transfers between devices with their start and end apart: 3, of which 3 were waited for; matrix products, arithmetic and copies ran while one was open for 7% of the time, Pallas kernels for 0%

commit v1 on v0

v1 whole, which is shorter than its diff:
```python
import functools

import jax
import jax.numpy as jnp
from jax import lax
from jax.experimental import pallas as pl
from jax.experimental.pallas import tpu as pltpu
from jax.sharding import PartitionSpec as P

QH = 64
KVH = 8
HD = 128
PREFIX = 128
BLOCK = 256
SCALE = HD ** (-0.5)


def dot(a, b, ca, cb):
    return lax.dot_general(a, b, (((ca,), (cb,)), ((), ())), preferred_element_type=jnp.float32)


def attention_kernel(d_ref, q_ref, k_ref, v_ref, pk_ref, pv_ref, *rest):
    dq_ref, dk_ref, dv_ref, prefix_ref, kall, vall, dk_acc, dv_acc = rest[-8:]
    h = pl.program_id(0)
    length = q_ref.shape[0]
    block = min(BLOCK, length)

    @pl.when(h == 0)
    def _():
        kall[:PREFIX, :] = pk_ref[...]
        kall[PREFIX:, :] = k_ref[...]
        vall[:PREFIX, :] = pv_ref[...]
        vall[PREFIX:, :] = v_ref[...]
        dk_acc[...] = jnp.zeros_like(dk_acc)
        dv_acc[...] = jnp.zeros_like(dv_acc)

    row = lax.broadcasted_iota(jnp.int32, (block, block), 0)
    col = lax.broadcasted_iota(jnp.int32, (block, block), 1)
    seen = row <= col
    for start in range(0, length, block):
        old = PREFIX + start
        total = old + block
        qb = q_ref[start : start + block, :]
        db = d_ref[start : start + block, :]
        keys = kall[:total, :]
        values = vall[:total, :]
        s = dot(keys, qb, 1, 1) * SCALE
        gp = dot(values, db, 1, 1)
        s = jnp.concatenate([s[:old], jnp.where(seen, s[old:], -jnp.inf)], axis=0)
        top = jnp.max(s, axis=0, keepdims=True)
        e = jnp.exp(s - top)
        p = e * (1.0 / jnp.sum(e, axis=0, keepdims=True))
        row_dot = jnp.sum(p * gp, axis=0, keepdims=True)
        g = (p * (gp - row_dot)).astype(jnp.bfloat16)
        p = p.astype(jnp.bfloat16)
        dq_ref[start : start + block, :] = (dot(g, keys, 0, 0) * SCALE).astype(dq_ref.dtype)
        dk_acc[:total, :] += dot(g, qb, 1, 0)
        dv_acc[:total, :] += dot(p, db, 1, 0)

    @pl.when(h == pl.num_programs(0) - 1)
    def _():
        dk = dk_acc[...] * SCALE
        dv = dv_acc[...]
        dk_ref[...] = dk[PREFIX:].astype(dk_ref.dtype)
        dv_ref[...] = dv[PREFIX:].astype(dv_ref.dtype)
        prefix_ref[:PREFIX, :] = dk[:PREFIX].astype(prefix_ref.dtype)
        prefix_ref[PREFIX:, :] = dv[:PREFIX].astype(prefix_ref.dtype)


def attention(c, d_attn, queries, keys, values, prefix_keys, prefix_values, held):
    length, wide = queries.shape
    kv_wide = keys.shape[1]
    group = QH // KVH
    at_head = pl.BlockSpec((length, HD), lambda h: (0, c * group + h))
    at_kv = pl.BlockSpec((length, HD), lambda h: (0, c))
    at_prefix = pl.BlockSpec((PREFIX, HD), lambda h: (0, c))
    in_specs = [pl.BlockSpec((length, HD), lambda h: (0, h)), at_head, at_kv, at_kv, at_prefix, at_prefix]
    aliases = {}
    if held:
        in_specs += [pl.BlockSpec(memory_space=pl.ANY)] * 3
        aliases = {6: 0, 7: 1, 8: 2}
    pairs = length * (PREFIX + length)
    return pl.pallas_call(
        attention_kernel,
        grid=(group,),
        in_specs=in_specs,
        out_specs=[at_head, at_kv, at_kv, pl.BlockSpec((2 * PREFIX, HD), lambda h: (0, 0))],
        out_shape=[
            jax.ShapeDtypeStruct((length, wide), jnp.bfloat16),
            jax.ShapeDtypeStruct((length, kv_wide), jnp.bfloat16),
            jax.ShapeDtypeStruct((length, kv_wide), jnp.bfloat16),
            jax.ShapeDtypeStruct((2 * PREFIX, HD), jnp.bfloat16),
        ],
        scratch_shapes=[
            pltpu.VMEM((PREFIX + length, HD), jnp.bfloat16),
            pltpu.VMEM((PREFIX + length, HD), jnp.bfloat16),
            pltpu.VMEM((PREFIX + length, HD), jnp.float32),
            pltpu.VMEM((PREFIX + length, HD), jnp.float32),
        ],
        input_output_aliases=aliases,
        compiler_params=pltpu.CompilerParams(vmem_limit_bytes=32 << 20),
        cost_estimate=pl.CostEstimate(
            flops=10 * group * pairs * HD, bytes_accessed=8 * length * group * HD, transcendentals=group * pairs
        ),
    )(d_attn, queries, keys, values, prefix_keys, prefix_values, *held)


def sum_over(x, axis, size):
    step = 1
    while step < size:
        other = lax.ppermute(x, axis, [(i, i ^ step) for i in range(size)])
        total = x.astype(jnp.float32) + other.astype(jnp.float32)
        step *= 2
        x = total.astype(jnp.bfloat16) if step < size else total
    return x.astype(jnp.float32)


def gather_rows(x, axis, size):
    rows = x.shape[0]
    me = lax.axis_index(axis)
    if size == 2:
        other = lax.ppermute(x, axis, [(0, 1), (1, 0)])
        first = me == 0
        return jnp.concatenate([jnp.where(first, x, other), jnp.where(first, other, x)], 0)
    return lax.all_gather(x, axis, axis=0, tiled=True)


def shards(n_dp, n_tensor, grad_out, out_weight, queries, keys, values, prefix_keys, prefix_values):
    full_rows = gather_rows(grad_out, "tensor", n_tensor)
    kv_local = keys.shape[1] // HD
    wide = QH // KVH * HD
    held = ()
    sums = []
    for c in range(kv_local):
        weight = lax.all_gather(out_weight[c * wide : (c + 1) * wide], "dp", axis=1, tiled=True)
        d_attn = dot(full_rows, weight, 1, 1).astype(jnp.bfloat16)
        *held, prefix = attention(c, d_attn, queries, keys, values, prefix_keys, prefix_values, held)
        sums.append(sum_over(prefix, "dp", n_dp))
    summed = jnp.concatenate(sums, axis=1)
    return (*held, summed[:PREFIX], summed[PREFIX:])


def solution(mesh):
    in_specs = (
        P(("dp", "tensor"), None),
        P("tensor", "dp"),
        P("dp", "tensor"),
        P("dp", "tensor"),
        P("dp", "tensor"),
        P(None, "tensor"),
        P(None, "tensor"),
    )
    out_specs = (
        P("dp", "tensor"),
        P("dp", "tensor"),
        P("dp", "tensor"),
        P(None, "tensor"),
        P(None, "tensor"),
    )
    body = functools.partial(shards, mesh.shape["dp"], mesh.shape["tensor"])
    return jax.shard_map(body, mesh=mesh, in_specs=in_specs, out_specs=out_specs, check_vma=False)
```

time: 717 us -> 601 us (0.84)
  matrix products: 126 us -> 59.5 us
  Pallas kernels: 0 us -> 58.4 us
  waiting for transfers between devices: 475 us -> 432 us
  local copies, waits for them, and re-layouts: 55.6 us -> 13.8 us
  other arithmetic: 45.2 us -> 6.11 us
  starting transfers between devices: 0.11 us -> 17.1 us
    ppermute x0 -> x17, waiting for transfers between devices: none -> 101 us  [the longest x1 90.9 us: gather_rows(): other = lax.ppermute(x, axis, [(0, 1), (1, 0)])]
    all_gather x2 -> x4, waiting for transfers between devices: 405 us -> 328 us  [shards(): lax.all_gather(out_weight[c * wide:(c + 1) * wide], 'dp', axis=1, tiled=T...]
    psum x1 -> x0, waiting for transfers between devices: 68.2 us -> none  [reduce_prefix(): lax.psum(key_part.astype(jnp.bfloat16), 'dp').astype(jnp.float32)]
    pallas_call x0 -> x4, Pallas kernels: none -> 58.4 us  [attention(): pl.pallas_call(attention_kernel, grid=(group,), in_specs=in_specs, out_sp...]
    dot_general x5 -> x4, matrix products: 104 us -> 59.5 us  [dot(): lax.dot_general(a, b, (((ca,), (cb,)), ((), ())), preferred_element_type=...]
    convert_element_type x3 -> x12, other arithmetic: 44.9 us -> 0.25 us  [sum_over(): x = total.astype(jnp.bfloat16) if step < size else total]
    convert_element_type x3 -> x0, local copies, waits for them, and re-layouts: 35.8 us -> none  [the longest x1 34.3 us: shards(): probs_low = probs.astype(jnp.bfloat16)]
    sub x1 -> x0, matrix products: 21.9 us -> none  [shards(): expo = jnp.exp(scores - top)]
  transfers between devices with their start and end apart: 3 -> 21, of which waited for: 3 -> 13; matrix products, arithmetic and copies ran while one was open for 7% -> 8% of each run, Pallas kernels for 0% -> 7%
where the time goes in v1:
time: 601 us
  waiting for transfers between devices  432 us (72%)
  matrix products  59.5 us (10%)
  Pallas kernels  58.4 us (10%)
  starting transfers between devices  17.1 us (3%)
  between operations  14 us (2%)
  local copies, waits for them, and re-layouts  13.8 us (2%)
  other arithmetic  6.11 us (1%)
    all_gather x4, waiting for transfers between devices, shards(): lax.all_gather(out_weight[c * wide:(c + 1) * wide], 'dp', axis=1, tiled=T...  328 us
    ppermute x1, waiting for transfers between devices, gather_rows(): other = lax.ppermute(x, axis, [(0, 1), (1, 0)])  90.9 us
    dot_general x4, matrix products, dot(): lax.dot_general(a, b, (((ca,), (cb,)), ((), ())), preferred_element_type=...  59.5 us
    pallas_call x4, Pallas kernels, attention(): pl.pallas_call(attention_kernel, grid=(group,), in_specs=in_specs, out_sp...  58.4 us
    ppermute x16, starting transfers between devices, sum_over(): other = lax.ppermute(x, axis, [(i, i ^ step) for i in range(size)])  13.9 us
  transfers between devices with their start and end apart: 21, of which 13 were waited for; matrix products, arithmetic and copies ran while one was open for 8% of the time, Pallas kernels for 7%

profile of v1, /device:TPU:0, one launch (start us, length us, event | category | flops | bytes accessed | tf_op | source)
XLA Modules:
  0.0 600.5 jit_solution(16614553155868833315)
XLA Ops:
  7.2 4.2 fusion
  11.5 0.7 all-gather.9.cloned.1.call-update
  12.3 0.7 all-gather.7.cloned.1.call-update
  13.0 0.5 all-gather.5.cloned.1.call-update
  13.5 3.0 collective-permute-start
  16.6 90.9 %collective-permute-done = bf16[256,8192]{1,0:T(8,128)(2,1)} collective-permute-done((bf16[256,8192]{1,0:T(8,128)(2,1)}, bf16[256,8192]{1,0:T(8,128)(2,1)}, u32[]{:S(2)}, u32[]{:S(2)}) %collective-permute-start) | collective-permute-done | bytes 4194336 | tf_op jit(solution)/shard_map/ppermute | solution.py:122
  107.5 5.8 broadcast_select_fusion.1
  113.2 31.5 %all-gather.11.cloned.1.call-done = bf16[1024,8192]{1,0:T(8,128)(2,1)} async-done(((bf16[1024,512]{1,0:T(8,128)(2,1)}), bf16[1024,8192]{1,0:T(8,128)(2,1)}) %all-gather.11.cloned.1.call-update) | async-done | bytes 16777232 | tf_op jit(solution)/shard_map/all_gather | solution.py:135
  144.7 15.0 %convolution_convert_fusion.d_ref = bf16[512,1024]{1,0:T(8,128)(2,1)S(1)} fusion(bf16[1024,8192]{1,0:T(8,128)(2,1)} %all-gather.11.cloned.1.call-done, bf16[256,8192]{1,0:T(8,128)(2,1)} %get-tuple-element.38, bf16[256,8192]{1,0:T(8,128)(2,1)} %get-tuple-element.37), kind=kOutput, calls=%fused_computation.3 | convolution fusion | flops 8607236096 | bytes 26214400 | tf_op jit(solution)/shard_map/dot_general | solution.py:19
  159.7 2.2 copy-done
  161.9 14.6 %shard_map.110 = (bf16[512,4096]{1,0:T(8,128)(2,1)}, bf16[512,512]{1,0:T(8,128)(2,1)}, bf16[512,512]{1,0:T(8,128)(2,1)}, bf16[256,128]{1,0:T(8,128)(2,1)S(1)}) custom-call(bf16[512,1024]{1,0:T(8,128)(2,1)S(1)} %convolution_convert_fusion.d_ref, bf16[512,4096]{1,0:T(8,128)(2,1)S(1)} %copy-done, bf16[512,512]{1,0:T(8,128)(2,1)S(1)} %copy-done.4, ...), custom_call_target="tpu_custom_call" | custom-call | flops 3355443200 | bytes 4194304 | tf_op jit(solution)/shard_map/pallas_call | solution.py:83
  176.4 98.9 %all-gather.9.cloned.1.call-done = bf16[1024,8192]{1,0:T(8,128)(2,1)} async-done(((bf16[1024,512]{1,0:T(8,128)(2,1)}), bf16[1024,8192]{1,0:T(8,128)(2,1)}) %all-gather.9.cloned.1.call-update) | async-done | bytes 16777232 | tf_op jit(solution)/shard_map/all_gather | solution.py:135
  275.4 14.8 %convolution_convert_fusion.1.d_ref = bf16[512,1024]{1,0:T(8,128)(2,1)S(1)} fusion(bf16[1024,8192]{1,0:T(8,128)(2,1)} %all-gather.9.cloned.1.call-done, bf16[256,8192]{1,0:T(8,128)(2,1)} %get-tuple-element.38, bf16[256,8192]{1,0:T(8,128)(2,1)} %get-tuple-element.37), kind=kOutput, calls=%fused_computation.4 | convolution fusion | flops 8607236096 | bytes 26214400 | tf_op jit(solution)/shard_map/dot_general | solution.py:19
  290.2 2.2 copy-done.1
  292.4 14.6 %shard_map.111 = (bf16[512,4096]{1,0:T(8,128)(2,1)}, bf16[512,512]{1,0:T(8,128)(2,1)}, bf16[512,512]{1,0:T(8,128)(2,1)}, bf16[256,128]{1,0:T(8,128)(2,1)S(1)}) custom-call(bf16[512,1024]{1,0:T(8,128)(2,1)S(1)} %convolution_convert_fusion.1.d_ref, bf16[512,4096]{1,0:T(8,128)(2,1)S(1)} %copy-done.1, ...), custom_call_target="tpu_custom_call", output_to_operand_aliasing={{0}: (6, {}), {1}: (7, {}), {2}: (8, {})} | custom-call | flops 3355443200 | bytes 4194304 | tf_op jit(solution)/shard_map/pallas_call | solution.py:83
  307.0 99.0 %all-gather.7.cloned.1.call-done = bf16[1024,8192]{1,0:T(8,128)(2,1)} async-done(((bf16[1024,512]{1,0:T(8,128)(2,1)}), bf16[1024,8192]{1,0:T(8,128)(2,1)}) %all-gather.7.cloned.1.call-update) | async-done | bytes 16777232 | tf_op jit(solution)/shard_map/all_gather | solution.py:135
  406.1 14.9 %convolution_convert_fusion.2.d_ref = bf16[512,1024]{1,0:T(8,128)(2,1)S(1)} fusion(bf16[1024,8192]{1,0:T(8,128)(2,1)} %all-gather.7.cloned.1.call-done, bf16[256,8192]{1,0:T(8,128)(2,1)} %get-tuple-element.38, bf16[256,8192]{1,0:T(8,128)(2,1)} %get-tuple-element.37), kind=kOutput, calls=%fused_computation.5 | convolution fusion | flops 8607236096 | bytes 26214400 | tf_op jit(solution)/shard_map/dot_general | solution.py:19
  421.0 2.2 copy-done.2
  423.1 14.6 %shard_map.112 = (bf16[512,4096]{1,0:T(8,128)(2,1)}, bf16[512,512]{1,0:T(8,128)(2,1)}, bf16[512,512]{1,0:T(8,128)(2,1)}, bf16[256,128]{1,0:T(8,128)(2,1)S(1)}) custom-call(bf16[512,1024]{1,0:T(8,128)(2,1)S(1)} %convolution_convert_fusion.2.d_ref, bf16[512,4096]{1,0:T(8,128)(2,1)S(1)} %copy-done.2, ...), custom_call_target="tpu_custom_call", output_to_operand_aliasing={{0}: (6, {}), {1}: (7, {}), {2}: (8, {})} | custom-call | flops 3355443200 | bytes 4194304 | tf_op jit(solution)/shard_map/pallas_call | solution.py:83
  437.8 98.9 %all-gather.5.cloned.1.call-done = bf16[1024,8192]{1,0:T(8,128)(2,1)} async-done(((bf16[1024,512]{1,0:T(8,128)(2,1)}), bf16[1024,8192]{1,0:T(8,128)(2,1)}) %all-gather.5.cloned.1.call-update) | async-done | bytes 16777232 | tf_op jit(solution)/shard_map/all_gather | solution.py:135
  536.7 14.9 %convolution_convert_fusion.3.d_ref = bf16[512,1024]{1,0:T(8,128)(2,1)S(1)} fusion(bf16[1024,8192]{1,0:T(8,128)(2,1)} %all-gather.5.cloned.1.call-done, bf16[256,8192]{1,0:T(8,128)(2,1)} %get-tuple-element.38, bf16[256,8192]{1,0:T(8,128)(2,1)} %get-tuple-element.37), kind=kOutput, calls=%fused_computation.6 | convolution fusion | flops 8607236096 | bytes 26214400 | tf_op jit(solution)/shard_map/dot_general | solution.py:19
  551.5 2.2 copy-done.3
  553.7 14.6 %shard_map.113 = (bf16[512,4096]{1,0:T(8,128)(2,1)}, bf16[512,512]{1,0:T(8,128)(2,1)}, bf16[512,512]{1,0:T(8,128)(2,1)}, bf16[256,128]{1,0:T(8,128)(2,1)S(1)}) custom-call(bf16[512,1024]{1,0:T(8,128)(2,1)S(1)} %convolution_convert_fusion.3.d_ref, bf16[512,4096]{1,0:T(8,128)(2,1)S(1)} %copy-done.3, ...), custom_call_target="tpu_custom_call", output_to_operand_aliasing={{0}: (6, {}), {1}: (7, {}), {2}: (8, {})} | custom-call | flops 3355443200 | bytes 4194304 | tf_op jit(solution)/shard_map/pallas_call | solution.py:83
  568.3 0.3 collective-permute-start.13
  568.6 0.3 collective-permute-start.9
  568.8 0.3 collective-permute-start.5
  569.1 0.3 collective-permute-start.1
  569.4 0.2 collective-permute-done.13
  569.6 1.5 collective-permute-start.14
  571.2 0.6 collective-permute-start.10
  571.8 1.5 collective-permute-start.6
  573.4 0.6 collective-permute-start.2
  574.0 0.2 collective-permute-done.14
  574.2 0.1 collective-permute-start.15
  574.3 1.9 collective-permute-done.10
  576.2 0.1 collective-permute-start.11
  576.4 1.1 collective-permute-done.6
  577.5 0.9 collective-permute-start.7
  578.4 1.2 collective-permute-start.3
  579.7 1.5 collective-permute-start.16
  581.2 1.5 collective-permute-start.12
  582.8 1.5 collective-permute-start.8
  584.4 1.5 collective-permute-start.4
  585.9 4.5 collective-permute-done.16
  590.4 1.3 collective-permute-done.12
  591.7 0.7 collective-permute-done.8
  592.4 0.7 collective-permute-done.4
  593.2 0.8 fusion.1
  (42 shorter events, 0.6 us)
Async XLA Ops:
  7.2 137.5 %all-gather.11.cloned.1.call-start = ((), (), s32[]{:S(2)}) async-start(), calls=%async_computation.3 | async-start | bytes 17825792 | tf_op jit(solution)/shard_map/all_gather | solution.py:135
  11.5 263.9 %all-gather.9.cloned.1.call-start = ((), (), s32[]{:S(2)}) async-start(), calls=%async_computation.2 | async-start | bytes 17825792 | tf_op jit(solution)/shard_map/all_gather | solution.py:135
  12.2 393.9 %all-gather.7.cloned.1.call-start = ((), (), s32[]{:S(2)}) async-start(), calls=%async_computation.1 | async-start | bytes 17825792 | tf_op jit(solution)/shard_map/all_gather | solution.py:135
  13.0 523.7 %all-gather.5.cloned.1.call-start = ((), (), s32[]{:S(2)}) async-start(), calls=%async_computation | async-start | bytes 17825792 | tf_op jit(solution)/shard_map/all_gather | solution.py:135
  13.5 93.9 %collective-permute-start = (bf16[256,8192]{1,0:T(8,128)(2,1)}, bf16[256,8192]{1,0:T(8,128)(2,1)}, u32[]{:S(2)}, u32[]{:S(2)}) collective-permute-start(bf16[256,8192]{1,0:T(8,128)(2,1)} %param.7), channel_id=1, source_target_pairs={{0,1},{1,0},{2,3},{3,2},{4,5},{5,4},{6,7},{7,6},{8,9},{9,8},{10,11... | collective-permute-start | bytes 12582920 | tf_op jit(solution)/shard_map/ppermute | solution.py:122
  144.7 15.0 %copy-start.4 = (bf16[512,512]{1,0:T(8,128)(2,1)S(1)}, bf16[512,512]{1,0:T(8,128)(2,1)}, u32[]{:S(2)}) copy-start(bf16[512,512]{1,0:T(8,128)(2,1)} %k_ref.7) | copy-start | bytes 1572868
  144.7 15.0 %copy-start.5 = (bf16[512,512]{1,0:T(8,128)(2,1)S(1)}, bf16[512,512]{1,0:T(8,128)(2,1)}, u32[]{:S(2)}) copy-start(bf16[512,512]{1,0:T(8,128)(2,1)} %v_ref.7) | copy-start | bytes 1572868
  144.7 15.0 %copy-start.6 = (bf16[128,512]{1,0:T(8,128)(2,1)S(1)}, bf16[128,512]{1,0:T(8,128)(2,1)}, u32[]{:S(2)}) copy-start(bf16[128,512]{1,0:T(8,128)(2,1)} %pk_ref.7) | copy-start | bytes 393220
  144.7 15.0 %copy-start.7 = (bf16[128,512]{1,0:T(8,128)(2,1)S(1)}, bf16[128,512]{1,0:T(8,128)(2,1)}, u32[]{:S(2)}) copy-start(bf16[128,512]{1,0:T(8,128)(2,1)} %pv_ref.7) | copy-start | bytes 393220
  159.7 2.2 copy-start
  290.2 2.2 copy-start.1
  421.0 2.2 copy-start.2
  551.5 2.2 copy-start.3
  568.3 1.3 collective-permute-start.13
  568.6 2.5 collective-permute-start.9
  568.8 3.0 collective-permute-start.5
  569.1 4.3 collective-permute-start.1
  569.6 4.6 collective-permute-start.14
  571.2 5.0 collective-permute-start.10
  571.8 5.6 collective-permute-start.6
  573.4 5.0 collective-permute-start.2
  574.2 5.5 collective-permute-start.15
  576.2 5.0 collective-permute-start.11
  577.5 5.3 collective-permute-start.7
  578.4 5.9 collective-permute-start.3
  579.7 10.7 %collective-permute-start.16 = (bf16[256,128]{1,0:T(8,128)(2,1)S(1)}, bf16[256,128]{1,0:T(8,128)(2,1)S(1)}, u32[]{:S(2)}, u32[]{:S(2)}) collective-permute-start(bf16[256,128]{1,0:T(8,128)(2,1)S(1)} %add_convert_fusion), channel_id=1, source_target_pairs={{0,16},{2,18},{4,20},{6,22},{8,24},{10,26},{12,28},{14,30},{16,0},... | collective-permute-start | bytes 196616 | tf_op jit(solution)/shard_map/ppermute | solution.py:111
  581.2 10.4 %collective-permute-start.12 = (bf16[256,128]{1,0:T(8,128)(2,1)S(1)}, bf16[256,128]{1,0:T(8,128)(2,1)S(1)}, u32[]{:S(2)}, u32[]{:S(2)}) collective-permute-start(bf16[256,128]{1,0:T(8,128)(2,1)S(1)} %add_convert_fusion.3), channel_id=1, source_target_pairs={{0,16},{2,18},{4,20},{6,22},{8,24},{10,26},{12,28},{14,30},{16,0},... | collective-permute-start | bytes 196616 | tf_op jit(solution)/shard_map/ppermute | solution.py:111
  582.8 9.6 %collective-permute-start.8 = (bf16[256,128]{1,0:T(8,128)(2,1)S(1)}, bf16[256,128]{1,0:T(8,128)(2,1)S(1)}, u32[]{:S(2)}, u32[]{:S(2)}) collective-permute-start(bf16[256,128]{1,0:T(8,128)(2,1)S(1)} %add_convert_fusion.6), channel_id=1, source_target_pairs={{0,16},{2,18},{4,20},{6,22},{8,24},{10,26},{12,28},{14,30},{16,0},... | collective-permute-start | bytes 196616 | tf_op jit(solution)/shard_map/ppermute | solution.py:111
  584.4 8.7 %collective-permute-start.4 = (bf16[256,128]{1,0:T(8,128)(2,1)S(1)}, bf16[256,128]{1,0:T(8,128)(2,1)S(1)}, u32[]{:S(2)}, u32[]{:S(2)}) collective-permute-start(bf16[256,128]{1,0:T(8,128)(2,1)S(1)} %add_convert_fusion.9), channel_id=1, source_target_pairs={{0,16},{2,18},{4,20},{6,22},{8,24},{10,26},{12,28},{14,30},{16,0},... | collective-permute-start | bytes 196616 | tf_op jit(solution)/shard_map/ppermute | solution.py:111
Sparse Core Ops, SparseCore 0:
  11.6 133.0 all-gather.10
  146.8 128.5 all-gather.8
  277.5 128.5 all-gather.6
  408.1 128.5 all-gather.4

commit v2 on v1

v2 whole, which is shorter than its diff:
```python
import functools

import jax
import jax.numpy as jnp
from jax import lax
from jax.experimental import pallas as pl
from jax.experimental.pallas import tpu as pltpu
from jax.sharding import PartitionSpec as P

QH = 64
KVH = 8
HD = 128
PREFIX = 128
BLOCK = 256
SCALE = HD ** (-0.5)


def dot(a, b, ca, cb):
    return lax.dot_general(a, b, (((ca,), (cb,)), ((), ())), preferred_element_type=jnp.float32)


def attention_kernel(g_ref, w_ref, q_ref, k_ref, v_ref, pk_ref, pv_ref, *rest):
    dq_ref, dk_ref, dv_ref, prefix_ref, kall, vall, dk_acc, dv_acc, d_buf = rest[-9:]
    pairs = QH // KVH * HD // q_ref.shape[1]
    step = lax.rem(pl.program_id(0), pairs)
    length = q_ref.shape[0]
    block = min(BLOCK, length)

    @pl.when(step == 0)
    def _():
        kall[:PREFIX, :] = pk_ref[...]
        kall[PREFIX:, :] = k_ref[...]
        vall[:PREFIX, :] = pv_ref[...]
        vall[PREFIX:, :] = v_ref[...]
        dk_acc[...] = jnp.zeros_like(dk_acc)
        dv_acc[...] = jnp.zeros_like(dv_acc)

    d_buf[...] = dot(g_ref[...], w_ref[...], 1, 1).astype(jnp.bfloat16)
    row = lax.broadcasted_iota(jnp.int32, (block, block), 0)
    col = lax.broadcasted_iota(jnp.int32, (block, block), 1)
    seen = row <= col
    for start in range(0, length, block):
        old = PREFIX + start
        total = old + block
        keys = kall[:total, :]
        values = vall[:total, :]
        for at in range(0, q_ref.shape[1], HD):
            qb = q_ref[start : start + block, at : at + HD]
            db = d_buf[start : start + block, at : at + HD]
            s = dot(keys, qb, 1, 1) * SCALE
            gp = dot(values, db, 1, 1)
            s = jnp.concatenate([s[:old], jnp.where(seen, s[old:], -jnp.inf)], axis=0)
            top = jnp.max(s, axis=0, keepdims=True)
            e = jnp.exp(s - top)
            p = e * (1.0 / jnp.sum(e, axis=0, keepdims=True))
            row_dot = jnp.sum(p * gp, axis=0, keepdims=True)
            g = (p * (gp - row_dot)).astype(jnp.bfloat16)
            p = p.astype(jnp.bfloat16)
            dq_ref[start : start + block, at : at + HD] = (dot(g, keys, 0, 0) * SCALE).astype(dq_ref.dtype)
            dk_acc[:total, :] += dot(g, qb, 1, 0)
            dv_acc[:total, :] += dot(p, db, 1, 0)

    @pl.when(step == pairs - 1)
    def _():
        dk = dk_acc[...] * SCALE
        dv = dv_acc[...]
        dk_ref[...] = dk[PREFIX:].astype(dk_ref.dtype)
        dv_ref[...] = dv[PREFIX:].astype(dv_ref.dtype)
        prefix_ref[:PREFIX, :] = dk[:PREFIX].astype(prefix_ref.dtype)
        prefix_ref[PREFIX:, :] = dv[:PREFIX].astype(prefix_ref.dtype)


def attention(first, rows, weight, queries, keys, values, prefix_keys, prefix_values, held):
    length, wide = queries.shape
    kv_wide = keys.shape[1]
    depth = rows.shape[1]
    pairs = QH // KVH // 2
    heads = weight.shape[0] // HD
    count = heads // (2 * pairs)
    at_pair = pl.BlockSpec((length, 2 * HD), lambda i: (0, first * pairs + i))
    at_kv = pl.BlockSpec((length, HD), lambda i: (0, first + i // pairs))
    at_prefix = pl.BlockSpec((PREFIX, HD), lambda i: (0, first + i // pairs))
    in_specs = [
        pl.BlockSpec((length, depth), lambda i: (0, 0), pipeline_mode=pl.Buffered(1)),
        pl.BlockSpec((2 * HD, depth), lambda i: (i, 0)),
        at_pair, at_kv, at_kv, at_prefix, at_prefix,
    ]
    aliases = {}
    if held:
        in_specs += [pl.BlockSpec(memory_space=pl.ANY)] * 3
        aliases = {7: 0, 8: 1, 9: 2}
    scores = heads * length * (PREFIX + length)
    return pl.pallas_call(
        attention_kernel,
        grid=(heads // 2,),
        in_specs=in_specs,
        out_specs=[at_pair, at_kv, at_kv, pl.BlockSpec((2 * PREFIX, HD), lambda i: (0, i // pairs))],
        out_shape=[
            jax.ShapeDtypeStruct((length, wide), jnp.bfloat16),
            jax.ShapeDtypeStruct((length, kv_wide), jnp.bfloat16),
            jax.ShapeDtypeStruct((length, kv_wide), jnp.bfloat16),
            jax.ShapeDtypeStruct((2 * PREFIX, count * HD), jnp.bfloat16),
        ],
        scratch_shapes=[
            pltpu.VMEM((PREFIX + length, HD), jnp.bfloat16),
            pltpu.VMEM((PREFIX + length, HD), jnp.bfloat16),
            pltpu.VMEM((PREFIX + length, HD), jnp.float32),
            pltpu.VMEM((PREFIX + length, HD), jnp.float32),
            pltpu.VMEM((length, 2 * HD), jnp.bfloat16),
        ],
        input_output_aliases=aliases,
        compiler_params=pltpu.CompilerParams(vmem_limit_bytes=48 << 20),
        cost_estimate=pl.CostEstimate(
            flops=10 * scores * HD + 2 * length * depth * heads * HD,
            bytes_accessed=2 * depth * (length + heads * HD),
            transcendentals=scores,
        ),
    )(rows, weight, queries, keys, values, prefix_keys, prefix_values, *held)


def sum_over(x, axis, size):
    step = 1
    while step < size:
        other = lax.ppermute(x, axis, [(i, i ^ step) for i in range(size)])
        total = x.astype(jnp.float32) + other.astype(jnp.float32)
        step *= 2
        x = total.astype(jnp.bfloat16) if step < size else total
    return x.astype(jnp.float32)


def gather_rows(x, axis, size):
    rows = x.shape[0]
    me = lax.axis_index(axis)
    if size == 2:
        other = lax.ppermute(x, axis, [(0, 1), (1, 0)])
        first = me == 0
        return jnp.concatenate([jnp.where(first, x, other), jnp.where(first, other, x)], 0)
    return lax.all_gather(x, axis, axis=0, tiled=True)


def shards(n_dp, n_tensor, grad_out, out_weight, queries, keys, values, prefix_keys, prefix_values):
    full_rows = gather_rows(grad_out, "tensor", n_tensor)
    kv_local = keys.shape[1] // HD
    wide = QH // KVH * HD
    parts = 2 if kv_local % 2 == 0 else 1
    count = kv_local // parts
    weights = [
        lax.all_gather(out_weight[c * count * wide : (c + 1) * count * wide], "dp", axis=1, tiled=True)
        for c in range(parts)
    ]
    held = ()
    sums = []
    for c in range(parts):
        weight = weights[c]
        if sums:
            weight, sums[-1] = lax.optimization_barrier((weight, sums[-1]))
        *held, prefix = attention(c * count, full_rows, weight, queries, keys, values, prefix_keys, prefix_values, held)
        sums.append(sum_over(prefix, "dp", n_dp))
    summed = jnp.concatenate(sums, axis=1)
    return (*held, summed[:PREFIX], summed[PREFIX:])


def solution(mesh):
    in_specs = (
        P(("dp", "tensor"), None),
        P("tensor", "dp"),
        P("dp", "tensor"),
        P("dp", "tensor"),
        P("dp", "tensor"),
        P(None, "tensor"),
        P(None, "tensor"),
    )
    out_specs = (
        P("dp", "tensor"),
        P("dp", "tensor"),
        P("dp", "tensor"),
        P(None, "tensor"),
        P(None, "tensor"),
    )
    body = functools.partial(shards, mesh.shape["dp"], mesh.shape["tensor"])
    return jax.shard_map(body, mesh=mesh, in_specs=in_specs, out_specs=out_specs, check_vma=False)
```

time: 601 us -> 452 us (0.75)
  waiting for transfers between devices: 432 us -> 273 us
  Pallas kernels: 58.4 us -> 128 us
  matrix products: 59.5 us -> 0 us
  other arithmetic: 6.11 us -> 15.7 us
    all_gather x4 -> x2, waiting for transfers between devices: 328 us -> 140 us  [shards(): lax.all_gather(out_weight[c * count * wide:(c + 1) * count * wide], 'dp',...]
    pallas_call x4 -> x2, Pallas kernels: 58.4 us -> 128 us  [attention(): pl.pallas_call(attention_kernel, grid=(heads // 2,), in_specs=in_specs, o...]
    dot_general x4 -> x0, matrix products: 59.5 us -> none  [dot(): lax.dot_general(a, b, (((ca,), (cb,)), ((), ())), preferred_element_type=...]
    ppermute x16 -> x8, waiting for transfers between devices: 10.5 us -> 41.6 us  [sum_over(): other = lax.ppermute(x, axis, [(i, i ^ step) for i in range(size)])]
    concatenate x0 -> x1, other arithmetic: none -> 8.09 us  [gather_rows(): jnp.concatenate([jnp.where(first, x, other), jnp.where(first, other, x)], 0)]
    ppermute x16 -> x8, starting transfers between devices: 13.9 us -> 8.86 us  [sum_over(): other = lax.ppermute(x, axis, [(i, i ^ step) for i in range(size)])]
  transfers between devices with their start and end apart: 21 -> 11, of which waited for: 13 -> 11; matrix products, arithmetic and copies ran while one was open for 8% -> 3% of each run, Pallas kernels for 7% -> 14%
where the time goes in v2:
time: 452 us
  waiting for transfers between devices  273 us (60%)
  Pallas kernels  128 us (28%)
  other arithmetic  15.7 us (3%)
  between operations  14.1 us (3%)
  starting transfers between devices  12 us (3%)
  local copies, waits for them, and re-layouts  8.93 us (2%)
    all_gather x2, waiting for transfers between devices, shards(): lax.all_gather(out_weight[c * count * wide:(c + 1) * count * wide], 'dp',...  140 us
    pallas_call x2, Pallas kernels, attention(): pl.pallas_call(attention_kernel, grid=(heads // 2,), in_specs=in_specs, o...  128 us
    ppermute x1, waiting for transfers between devices, gather_rows(): other = lax.ppermute(x, axis, [(0, 1), (1, 0)])  90.9 us
    ppermute x8, waiting for transfers between devices, sum_over(): other = lax.ppermute(x, axis, [(i, i ^ step) for i in range(size)])  41.6 us
  transfers between devices with their start and end apart: 11, of which 11 were waited for; matrix products, arithmetic and copies ran while one was open for 3% of the time, Pallas kernels for 14%

profile of v2, /device:TPU:0, one launch (start us, length us, event | category | flops | bytes accessed | tf_op | source)
XLA Modules:
  0.0 451.8 jit_solution(18118551385351675377)
XLA Ops:
  7.2 0.0 all-gather.5.cloned.1.call-start
  7.2 4.5 %fusion.1 = (bf16[2048,512]{1,0:T(8,128)(2,1)}, bf16[2048,512]{1,0:T(8,128)(2,1)}) fusion(bf16[4096,512]{1,0:T(8,128)(2,1)} %param.8), kind=kLoop, calls=%fused_computation.15 | loop fusion | bytes 8388608 | tf_op jit(solution)/shard_map/slice | solution.py:148
  11.8 0.0 all-gather.5.cloned.1.call-update
  11.8 0.0 all-gather.3.cloned.1.call-start
  11.8 0.7 all-gather.3.cloned.1.call-update
  12.5 3.0 collective-permute-start
  15.6 90.9 %collective-permute-done = bf16[256,8192]{1,0:T(8,128)(2,1)} collective-permute-done((bf16[256,8192]{1,0:T(8,128)(2,1)}, bf16[256,8192]{1,0:T(8,128)(2,1)}, u32[]{:S(2)}, u32[]{:S(2)}) %collective-permute-start) | collective-permute-done | bytes 4194336 | tf_op jit(solution)/shard_map/ppermute | solution.py:135
  106.5 6.5 %broadcast_select_fusion.1 = (bf16[256,8192]{1,0:T(8,128)(2,1)}, bf16[256,8192]{1,0:T(8,128)(2,1)}) fusion(bf16[256,8192]{1,0:T(8,128)(2,1)} %param.7, bf16[256,8192]{1,0:T(8,128)(2,1)} %collective-permute-done, pred[]{:T(512)S(6)} %eq.3), kind=kLoop, calls=%fused_computation.2 | loop fusion | flops 4194304 | bytes 16777216 | tf_op jit(solution)/shard_map/jit(_where)/select_n | solution.py:137
  112.9 0.0 copy-start.2
  112.9 0.0 copy-start.3
  112.9 0.0 copy-start.4
  112.9 0.0 copy-start.5
  112.9 8.1 %pad_maximum_fusion.g_ref = bf16[512,8192]{1,0:T(8,128)(2,1)} fusion(bf16[256,8192]{1,0:T(8,128)(2,1)} %get-tuple-element.26, bf16[256,8192]{1,0:T(8,128)(2,1)} %get-tuple-element.25), kind=kLoop, calls=%fused_computation | loop fusion | flops 16777216 | bytes 16777216 | tf_op jit(solution)/shard_map/concatenate | solution.py:137
  121.0 61.7 %all-gather.5.cloned.1.call-done.w_ref = bf16[2048,8192]{1,0:T(8,128)(2,1)} async-done(((bf16[2048,512]{1,0:T(8,128)(2,1)}), bf16[2048,8192]{1,0:T(8,128)(2,1)}) %all-gather.5.cloned.1.call-update) | async-done | bytes 33554448 | tf_op jit(solution)/shard_map/all_gather | solution.py:148
  182.7 0.0 copy-done.2
  182.7 0.0 copy-done.3
  182.7 0.0 copy-done.4
  182.7 0.0 copy-done.5
  182.7 0.0 copy-start
  182.7 2.2 copy-done
  184.9 64.1 %shard_map.110 = (bf16[512,4096]{1,0:T(8,128)(2,1)}, bf16[512,512]{1,0:T(8,128)(2,1)}, bf16[512,512]{1,0:T(8,128)(2,1)}, bf16[256,256]{1,0:T(8,128)(2,1)S(1)}) custom-call(bf16[512,8192]{1,0:T(8,128)(2,1)} %pad_maximum_fusion.g_ref, bf16[2048,8192]{1,0:T(8,128)(2,1)} %all-gather.5.cloned.1.call-done.w_ref, bf16[512,4096]{1,0:T(8,128)(2,1)S(1)} %copy-done, ...), custom_call_target="tpu_custom_call" | custom-call | flops 23890755584 | bytes 41943040 | tf_op jit(solution)/shard_map/pallas_call | solution.py:93
  249.1 0.3 collective-permute-start.1
  249.3 1.3 collective-permute-done.1
  250.6 1.0 collective-permute-start.2
  251.6 7.9 %collective-permute-done.2 = bf16[256,256]{1,0:T(8,128)(2,1)S(1)} collective-permute-done((bf16[256,256]{1,0:T(8,128)(2,1)S(1)}, bf16[256,256]{1,0:T(8,128)(2,1)S(1)}, u32[]{:S(2)}, u32[]{:S(2)}) %collective-permute-start.2) | collective-permute-done | bytes 131104 | tf_op jit(solution)/shard_map/ppermute | solution.py:124
  259.6 0.1 collective-permute-start.3
  259.7 8.6 %collective-permute-done.3 = bf16[256,256]{1,0:T(8,128)(2,1)S(1)} collective-permute-done((bf16[256,256]{1,0:T(8,128)(2,1)S(1)}, bf16[256,256]{1,0:T(8,128)(2,1)S(1)}, u32[]{:S(2)}, u32[]{:S(2)}) %collective-permute-start.3) | collective-permute-done | bytes 131104 | tf_op jit(solution)/shard_map/ppermute | solution.py:124
  268.3 2.0 collective-permute-start.4
  270.3 9.8 %collective-permute-done.4 = bf16[256,256]{1,0:T(8,128)(2,1)S(1)} collective-permute-done((bf16[256,256]{1,0:T(8,128)(2,1)S(1)}, bf16[256,256]{1,0:T(8,128)(2,1)S(1)}, u32[]{:S(2)}, u32[]{:S(2)}) %collective-permute-start.4) | collective-permute-done | bytes 131104 | tf_op jit(solution)/shard_map/ppermute | solution.py:124
  280.1 77.8 %all-gather.3.cloned.1.call-done.w_ref = bf16[2048,8192]{1,0:T(8,128)(2,1)} async-done(((bf16[2048,512]{1,0:T(8,128)(2,1)}), bf16[2048,8192]{1,0:T(8,128)(2,1)}) %all-gather.3.cloned.1.call-update) | async-done | bytes 33554448 | tf_op jit(solution)/shard_map/all_gather | solution.py:148
  358.0 0.0 copy-start.1
  358.0 2.2 copy-done.1
  360.1 64.2 %shard_map.111 = (bf16[512,4096]{1,0:T(8,128)(2,1)}, bf16[512,512]{1,0:T(8,128)(2,1)}, bf16[512,512]{1,0:T(8,128)(2,1)}, bf16[256,256]{1,0:T(8,128)(2,1)S(1)}) custom-call(bf16[512,8192]{1,0:T(8,128)(2,1)} %pad_maximum_fusion.g_ref, ...), custom_call_target="tpu_custom_call", output_to_operand_aliasing={{0}: (7, {}), {1}: (8, {}), {2}: (9, {})} | custom-call | flops 23890755584 | bytes 41943040 | tf_op jit(solution)/shard_map/pallas_call | solution.py:93
  424.4 0.3 collective-permute-start.5
  424.6 1.1 collective-permute-done.5
  425.8 1.2 collective-permute-start.6
  427.0 4.5 collective-permute-done.6
  431.5 1.6 collective-permute-start.7
  433.1 3.5 collective-permute-done.7
  436.6 2.5 collective-permute-start.8
  439.1 5.0 %collective-permute-done.8 = bf16[256,256]{1,0:T(8,128)(2,1)S(1)} collective-permute-done((bf16[256,256]{1,0:T(8,128)(2,1)S(1)}, bf16[256,256]{1,0:T(8,128)(2,1)S(1)}, u32[]{:S(2)}, u32[]{:S(2)}) %collective-permute-start.8) | collective-permute-done | bytes 131104 | tf_op jit(solution)/shard_map/ppermute | solution.py:124
  444.1 0.9 pad_maximum_fusion.1
  (8 shorter events, 0.3 us)
Async XLA Ops:
  7.2 175.5 %all-gather.5.cloned.1.call-start = ((), (), s32[]{:S(2)}) async-start(), calls=%async_computation.1 | async-start | bytes 35651584 | tf_op jit(solution)/shard_map/all_gather | solution.py:148
  11.8 346.2 %all-gather.3.cloned.1.call-start = ((), (), s32[]{:S(2)}) async-start(), calls=%async_computation | async-start | bytes 35651584 | tf_op jit(solution)/shard_map/all_gather | solution.py:148
  12.5 93.9 %collective-permute-start = (bf16[256,8192]{1,0:T(8,128)(2,1)}, bf16[256,8192]{1,0:T(8,128)(2,1)}, u32[]{:S(2)}, u32[]{:S(2)}) collective-permute-start(bf16[256,8192]{1,0:T(8,128)(2,1)} %param.7), channel_id=1, source_target_pairs={{0,1},{1,0},{2,3},{3,2},{4,5},{5,4},{6,7},{7,6},{8,9},{9,8},{10,11... | collective-permute-start | bytes 12582920 | tf_op jit(solution)/shard_map/ppermute | solution.py:135
  112.9 69.8 %copy-start.2 = (bf16[512,512]{1,0:T(8,128)(2,1)S(1)}, bf16[512,512]{1,0:T(8,128)(2,1)}, u32[]{:S(2)}) copy-start(bf16[512,512]{1,0:T(8,128)(2,1)} %k_ref.3) | copy-start | bytes 1572868
  112.9 69.8 %copy-start.3 = (bf16[512,512]{1,0:T(8,128)(2,1)S(1)}, bf16[512,512]{1,0:T(8,128)(2,1)}, u32[]{:S(2)}) copy-start(bf16[512,512]{1,0:T(8,128)(2,1)} %v_ref.3) | copy-start | bytes 1572868
  112.9 69.8 %copy-start.4 = (bf16[128,512]{1,0:T(8,128)(2,1)S(1)}, bf16[128,512]{1,0:T(8,128)(2,1)}, u32[]{:S(2)}) copy-start(bf16[128,512]{1,0:T(8,128)(2,1)} %pk_ref.3) | copy-start | bytes 393220
  112.9 69.8 %copy-start.5 = (bf16[128,512]{1,0:T(8,128)(2,1)S(1)}, bf16[128,512]{1,0:T(8,128)(2,1)}, u32[]{:S(2)}) copy-start(bf16[128,512]{1,0:T(8,128)(2,1)} %pv_ref.3) | copy-start | bytes 393220
  182.7 2.2 copy-start
  249.1 1.5 collective-permute-start.1
  250.6 8.9 %collective-permute-start.2 = (bf16[256,256]{1,0:T(8,128)(2,1)S(1)}, bf16[256,256]{1,0:T(8,128)(2,1)S(1)}, u32[]{:S(2)}, u32[]{:S(2)}) collective-permute-start(bf16[256,256]{1,0:T(8,128)(2,1)S(1)} %add_convert_fusion.5), channel_id=1, source_target_pairs={{0,4},{2,6},{4,0},{6,2},{8,12},{10,14},{12,8},{14,10},{16,20},{18,... | collective-permute-start | bytes 393224 | tf_op jit(solution)/shard_map/ppermute | solution.py:124
  259.6 8.7 %collective-permute-start.3 = (bf16[256,256]{1,0:T(8,128)(2,1)S(1)}, bf16[256,256]{1,0:T(8,128)(2,1)S(1)}, u32[]{:S(2)}, u32[]{:S(2)}) collective-permute-start(bf16[256,256]{1,0:T(8,128)(2,1)S(1)} %add_convert_fusion.4), channel_id=1, source_target_pairs={{0,8},{2,10},{4,12},{6,14},{8,0},{10,2},{12,4},{14,6},{16,24},{18,... | collective-permute-start | bytes 393224 | tf_op jit(solution)/shard_map/ppermute | solution.py:124
  268.3 11.8 %collective-permute-start.4 = (bf16[256,256]{1,0:T(8,128)(2,1)S(1)}, bf16[256,256]{1,0:T(8,128)(2,1)S(1)}, u32[]{:S(2)}, u32[]{:S(2)}) collective-permute-start(bf16[256,256]{1,0:T(8,128)(2,1)S(1)} %add_convert_fusion.3), channel_id=1, source_target_pairs={{0,16},{2,18},{4,20},{6,22},{8,24},{10,26},{12,28},{14,30},{16,0},... | collective-permute-start | bytes 393224 | tf_op jit(solution)/shard_map/ppermute | solution.py:124
  358.0 2.2 copy-start.1
  424.4 1.3 collective-permute-start.5
  425.8 5.7 %collective-permute-start.6 = (bf16[256,256]{1,0:T(8,128)(2,1)S(1)}, bf16[256,256]{1,0:T(8,128)(2,1)S(1)}, u32[]{:S(2)}, u32[]{:S(2)}) collective-permute-start(bf16[256,256]{1,0:T(8,128)(2,1)S(1)} %add_convert_fusion.2), channel_id=1, source_target_pairs={{0,4},{2,6},{4,0},{6,2},{8,12},{10,14},{12,8},{14,10},{16,20},{18,... | collective-permute-start | bytes 393224 | tf_op jit(solution)/shard_map/ppermute | solution.py:124
  431.5 5.0 %collective-permute-start.7 = (bf16[256,256]{1,0:T(8,128)(2,1)S(1)}, bf16[256,256]{1,0:T(8,128)(2,1)S(1)}, u32[]{:S(2)}, u32[]{:S(2)}) collective-permute-start(bf16[256,256]{1,0:T(8,128)(2,1)S(1)} %add_convert_fusion.1), channel_id=1, source_target_pairs={{0,8},{2,10},{4,12},{6,14},{8,0},{10,2},{12,4},{14,6},{16,24},{18,... | collective-permute-start | bytes 393224 | tf_op jit(solution)/shard_map/ppermute | solution.py:124
  436.6 7.5 %collective-permute-start.8 = (bf16[256,256]{1,0:T(8,128)(2,1)S(1)}, bf16[256,256]{1,0:T(8,128)(2,1)S(1)}, u32[]{:S(2)}, u32[]{:S(2)}) collective-permute-start(bf16[256,256]{1,0:T(8,128)(2,1)S(1)} %add_convert_fusion), channel_id=1, source_target_pairs={{0,16},{2,18},{4,20},{6,22},{8,24},{10,26},{12,28},{14,30},{16,0},... | collective-permute-start | bytes 393224 | tf_op jit(solution)/shard_map/ppermute | solution.py:124
Sparse Core Ops, SparseCore 0:
  11.9 170.7 all-gather.4
  184.2 173.6 all-gather.2

commit v3 on v2

--- a/solution.py
+++ b/solution.py
@@ -19,8 +19,8 @@
     return lax.dot_general(a, b, (((ca,), (cb,)), ((), ())), preferred_element_type=jnp.float32)
 
 
-def attention_kernel(g_ref, w_ref, q_ref, k_ref, v_ref, pk_ref, pv_ref, *rest):
-    dq_ref, dk_ref, dv_ref, prefix_ref, kall, vall, dk_acc, dv_acc, d_buf = rest[-9:]
+def attention_kernel(d_ref, q_ref, k_ref, v_ref, pk_ref, pv_ref, *rest):
+    dq_ref, dk_ref, dv_ref, prefix_ref, kall, vall, dk_acc, dv_acc = rest[-8:]
     pairs = QH // KVH * HD // q_ref.shape[1]
     step = lax.rem(pl.program_id(0), pairs)
     length = q_ref.shape[0]
@@ -35,7 +35,6 @@
         dk_acc[...] = jnp.zeros_like(dk_acc)
         dv_acc[...] = jnp.zeros_like(dv_acc)
 
-    d_buf[...] = dot(g_ref[...], w_ref[...], 1, 1).astype(jnp.bfloat16)
     row = lax.broadcasted_iota(jnp.int32, (block, block), 0)
     col = lax.broadcasted_iota(jnp.int32, (block, block), 1)
     seen = row <= col
@@ -46,7 +45,7 @@
         values = vall[:total, :]
         for at in range(0, q_ref.shape[1], HD):
             qb = q_ref[start : start + block, at : at + HD]
-            db = d_buf[start : start + block, at : at + HD]
+            db = d_ref[start : start + block, at : at + HD]
             s = dot(keys, qb, 1, 1) * SCALE
             gp = dot(values, db, 1, 1)
             s = jnp.concatenate([s[:old], jnp.where(seen, s[old:], -jnp.inf)], axis=0)
@@ -70,25 +69,23 @@
         prefix_ref[PREFIX:, :] = dv[:PREFIX].astype(prefix_ref.dtype)
 
 
-def attention(first, rows, weight, queries, keys, values, prefix_keys, prefix_values, held):
+def attention(first, d_attn, queries, keys, values, prefix_keys, prefix_values, held):
     length, wide = queries.shape
     kv_wide = keys.shape[1]
-    depth = rows.shape[1]
     pairs = QH // KVH // 2
-    heads = weight.shape[0] // HD
+    heads = d_attn.shape[1] // HD
     count = heads // (2 * pairs)
     at_pair = pl.BlockSpec((length, 2 * HD), lambda i: (0, first * pairs + i))
     at_kv = pl.BlockSpec((length, HD), lambda i: (0, first + i // pairs))
     at_prefix = pl.BlockSpec((PREFIX, HD), lambda i: (0, first + i // pairs))
     in_specs = [
-        pl.BlockSpec((length, depth), lambda i: (0, 0), pipeline_mode=pl.Buffered(1)),
-        pl.BlockSpec((2 * HD, depth), lambda i: (i, 0)),
+        pl.BlockSpec((length, 2 * HD), lambda i: (0, i)),
         at_pair, at_kv, at_kv, at_prefix, at_prefix,
     ]
     aliases = {}
     if held:
         in_specs += [pl.BlockSpec(memory_space=pl.ANY)] * 3
-        aliases = {7: 0, 8: 1, 9: 2}
+        aliases = {6: 0, 7: 1, 8: 2}
     scores = heads * length * (PREFIX + length)
     return pl.pallas_call(
         attention_kernel,
@@ -106,16 +103,15 @@
             pltpu.VMEM((PREFIX + length, HD), jnp.bfloat16),
             pltpu.VMEM((PREFIX + length, HD), jnp.float32),
             pltpu.VMEM((PREFIX + length, HD), jnp.float32),
-            pltpu.VMEM((length, 2 * HD), jnp.bfloat16),
         ],
         input_output_aliases=aliases,
-        compiler_params=pltpu.CompilerParams(vmem_limit_bytes=48 << 20),
+        compiler_params=pltpu.CompilerParams(vmem_limit_bytes=32 << 20),
         cost_estimate=pl.CostEstimate(
-            flops=10 * scores * HD + 2 * length * depth * heads * HD,
-            bytes_accessed=2 * depth * (length + heads * HD),
+            flops=10 * scores * HD,
+            bytes_accessed=8 * length * heads * HD,
             transcendentals=scores,
         ),
-    )(rows, weight, queries, keys, values, prefix_keys, prefix_values, *held)
+    )(d_attn, queries, keys, values, prefix_keys, prefix_values, *held)
 
 
 def sum_over(x, axis, size):
@@ -154,7 +150,8 @@
         weight = weights[c]
         if sums:
             weight, sums[-1] = lax.optimization_barrier((weight, sums[-1]))
-        *held, prefix = attention(c * count, full_rows, weight, queries, keys, values, prefix_keys, prefix_values, held)
+        d_attn = dot(full_rows, weight, 1, 1).astype(jnp.bfloat16)
+        *held, prefix = attention(c * count, d_attn, queries, keys, values, prefix_keys, prefix_values, held)
         sums.append(sum_over(prefix, "dp", n_dp))
     summed = jnp.concatenate(sums, axis=1)
     return (*held, summed[:PREFIX], summed[PREFIX:])

time: 452 us -> 438 us (0.969)
  Pallas kernels: 128 us -> 52 us
  matrix products: 0 us -> 47.9 us
  waiting for transfers between devices: 273 us -> 294 us
  other arithmetic: 15.7 us -> 8.27 us
    pallas_call x2, Pallas kernels: 128 us -> 52 us  [attention(): pl.pallas_call(attention_kernel, grid=(heads // 2,), in_specs=in_specs, o...]
    dot_general x0 -> x2, matrix products: none -> 47.9 us  [dot(): lax.dot_general(a, b, (((ca,), (cb,)), ((), ())), preferred_element_type=...]
    all_gather x2, waiting for transfers between devices: 140 us -> 161 us  [shards(): lax.all_gather(out_weight[c * count * wide:(c + 1) * count * wide], 'dp',...]
    concatenate x1 -> x0, other arithmetic: 8.09 us -> none  [gather_rows(): jnp.concatenate([jnp.where(first, x, other), jnp.where(first, other, x)], 0)]
  transfers between devices with their start and end apart: 11 -> 11, of which waited for: 11 -> 11; matrix products, arithmetic and copies ran while one was open for 3% -> 7% of each run, Pallas kernels for 14% -> 6%
where the time goes in v3:
time: 438 us
  waiting for transfers between devices  294 us (67%)
  Pallas kernels  52 us (12%)
  matrix products  47.9 us (11%)
  between operations  14.2 us (3%)
  starting transfers between devices  12.1 us (3%)
  local copies, waits for them, and re-layouts  9.02 us (2%)
  other arithmetic  8.27 us (2%)
    all_gather x2, waiting for transfers between devices, shards(): lax.all_gather(out_weight[c * count * wide:(c + 1) * count * wide], 'dp',...  161 us
    ppermute x1, waiting for transfers between devices, gather_rows(): other = lax.ppermute(x, axis, [(0, 1), (1, 0)])  90.9 us
    pallas_call x2, Pallas kernels, attention(): pl.pallas_call(attention_kernel, grid=(heads // 2,), in_specs=in_specs, o...  52 us
    dot_general x2, matrix products, dot(): lax.dot_general(a, b, (((ca,), (cb,)), ((), ())), preferred_element_type=...  47.9 us
    ppermute x8, waiting for transfers between devices, sum_over(): other = lax.ppermute(x, axis, [(i, i ^ step) for i in range(size)])  41.4 us
    ppermute x8, starting transfers between devices, sum_over(): other = lax.ppermute(x, axis, [(i, i ^ step) for i in range(size)])  9.02 us
  transfers between devices with their start and end apart: 11, of which 11 were waited for; matrix products, arithmetic and copies ran while one was open for 7% of the time, Pallas kernels for 6%

profile of v3, /device:TPU:0, one launch (start us, length us, event | category | flops | bytes accessed | tf_op | source)
XLA Modules:
  0.0 437.6 jit_solution(2436853423796676798)
XLA Ops:
  7.2 0.0 all-gather.5.cloned.1.call-start
  7.2 4.6 %fusion.7 = (bf16[2048,512]{1,0:T(8,128)(2,1)}, bf16[2048,512]{1,0:T(8,128)(2,1)}) fusion(bf16[4096,512]{1,0:T(8,128)(2,1)} %param.8), kind=kLoop, calls=%fused_computation.21 | loop fusion | bytes 8388608 | tf_op jit(solution)/shard_map/slice | solution.py:144
  11.8 0.0 all-gather.5.cloned.1.call-update
  11.8 0.0 all-gather.3.cloned.1.call-start
  11.9 0.7 all-gather.3.cloned.1.call-update
  12.6 3.0 collective-permute-start
  15.6 90.9 %collective-permute-done = bf16[256,8192]{1,0:T(8,128)(2,1)} collective-permute-done((bf16[256,8192]{1,0:T(8,128)(2,1)}, bf16[256,8192]{1,0:T(8,128)(2,1)}, u32[]{:S(2)}, u32[]{:S(2)}) %collective-permute-start) | collective-permute-done | bytes 4194336 | tf_op jit(solution)/shard_map/ppermute | solution.py:131
  106.5 6.5 %broadcast_select_fusion.1 = (bf16[256,8192]{1,0:T(8,128)(2,1)}, bf16[256,8192]{1,0:T(8,128)(2,1)}) fusion(bf16[256,8192]{1,0:T(8,128)(2,1)} %param.7, bf16[256,8192]{1,0:T(8,128)(2,1)} %collective-permute-done, pred[]{:T(512)S(6)} %eq.3), kind=kLoop, calls=%fused_computation.4 | loop fusion | flops 4194304 | bytes 16777216 | tf_op jit(solution)/shard_map/jit(_where)/select_n | solution.py:133
  112.9 69.8 %all-gather.5.cloned.1.call-done = bf16[2048,8192]{1,0:T(8,128)(2,1)} async-done(((bf16[2048,512]{1,0:T(8,128)(2,1)}), bf16[2048,8192]{1,0:T(8,128)(2,1)}) %all-gather.5.cloned.1.call-update) | async-done | bytes 33554448 | tf_op jit(solution)/shard_map/all_gather | solution.py:144
  182.7 0.0 copy-start.2
  182.7 0.0 copy-start.3
  182.7 0.0 copy-start.4
  182.7 0.0 copy-start.5
  182.7 24.0 %fusion.2.d_ref = bf16[512,2048]{1,0:T(8,128)(2,1)S(1)} fusion(bf16[2048,8192]{1,0:T(8,128)(2,1)} %all-gather.5.cloned.1.call-done, bf16[256,8192]{1,0:T(8,128)(2,1)} %get-tuple-element.26, bf16[256,8192]{1,0:T(8,128)(2,1)} %get-tuple-element.25), kind=kOutput, calls=%fused_computation.5 | convolution fusion | flops 17197694976 | bytes 44040192 | tf_op jit(solution)/shard_map/dot_general | solution.py:19
  206.8 0.0 copy-done.2
  206.8 0.0 copy-done.3
  206.8 0.0 copy-done.4
  206.8 0.0 copy-done.5
  206.8 0.0 copy-start
  206.8 2.2 copy-done
  209.1 25.9 %shard_map.110 = (bf16[512,4096]{1,0:T(8,128)(2,1)}, bf16[512,512]{1,0:T(8,128)(2,1)}, bf16[512,512]{1,0:T(8,128)(2,1)}, bf16[256,256]{1,0:T(8,128)(2,1)S(1)}) custom-call(bf16[512,2048]{1,0:T(8,128)(2,1)S(1)} %fusion.2.d_ref, bf16[512,4096]{1,0:T(8,128)(2,1)S(1)} %copy-done, bf16[512,512]{1,0:T(8,128)(2,1)S(1)} %copy-done.2, ...), custom_call_target="tpu_custom_call" | custom-call | flops 6710886400 | bytes 8388608 | tf_op jit(solution)/shard_map/pallas_call | solution.py:90
  235.0 0.2 collective-permute-start.1
  235.2 1.1 collective-permute-done.1
  236.4 1.2 collective-permute-start.2
  237.6 7.8 %collective-permute-done.2 = bf16[256,256]{1,0:T(8,128)(2,1)S(1)} collective-permute-done((bf16[256,256]{1,0:T(8,128)(2,1)S(1)}, bf16[256,256]{1,0:T(8,128)(2,1)S(1)}, u32[]{:S(2)}, u32[]{:S(2)}) %collective-permute-start.2) | collective-permute-done | bytes 131104 | tf_op jit(solution)/shard_map/ppermute | solution.py:120
  245.4 0.1 collective-permute-start.3
  245.5 8.6 %collective-permute-done.3 = bf16[256,256]{1,0:T(8,128)(2,1)S(1)} collective-permute-done((bf16[256,256]{1,0:T(8,128)(2,1)S(1)}, bf16[256,256]{1,0:T(8,128)(2,1)S(1)}, u32[]{:S(2)}, u32[]{:S(2)}) %collective-permute-start.3) | collective-permute-done | bytes 131104 | tf_op jit(solution)/shard_map/ppermute | solution.py:120
  254.1 2.0 collective-permute-start.4
  256.2 9.8 %collective-permute-done.4 = bf16[256,256]{1,0:T(8,128)(2,1)S(1)} collective-permute-done((bf16[256,256]{1,0:T(8,128)(2,1)S(1)}, bf16[256,256]{1,0:T(8,128)(2,1)S(1)}, u32[]{:S(2)}, u32[]{:S(2)}) %collective-permute-start.4) | collective-permute-done | bytes 131104 | tf_op jit(solution)/shard_map/ppermute | solution.py:120
  266.0 0.7 convert_add_fusion.1
  266.7 91.3 %all-gather.3.cloned.1.call-done = bf16[2048,8192]{1,0:T(8,128)(2,1)} async-done(((bf16[2048,512]{1,0:T(8,128)(2,1)}), bf16[2048,8192]{1,0:T(8,128)(2,1)}) %all-gather.3.cloned.1.call-update) | async-done | bytes 33554448 | tf_op jit(solution)/shard_map/all_gather | solution.py:144
  358.0 23.9 %fusion.3.d_ref = bf16[512,2048]{1,0:T(8,128)(2,1)S(1)} fusion(bf16[2048,8192]{1,0:T(8,128)(2,1)} %all-gather.3.cloned.1.call-done, bf16[256,8192]{1,0:T(8,128)(2,1)} %get-tuple-element.26, bf16[256,8192]{1,0:T(8,128)(2,1)} %get-tuple-element.25), kind=kOutput, calls=%fused_computation.6 | convolution fusion | flops 17197694976 | bytes 44040192 | tf_op jit(solution)/shard_map/dot_general | solution.py:19
  381.9 0.0 copy-start.1
  381.9 2.2 copy-done.1
  384.1 0.0 copy-start.6
  384.1 26.0 %shard_map.111 = (bf16[512,4096]{1,0:T(8,128)(2,1)}, bf16[512,512]{1,0:T(8,128)(2,1)}, bf16[512,512]{1,0:T(8,128)(2,1)}, bf16[256,256]{1,0:T(8,128)(2,1)S(1)}) custom-call(bf16[512,2048]{1,0:T(8,128)(2,1)S(1)} %fusion.3.d_ref, bf16[512,4096]{1,0:T(8,128)(2,1)S(1)} %copy-done.1, ...), custom_call_target="tpu_custom_call", output_to_operand_aliasing={{0}: (6, {}), {1}: (7, {}), {2}: (8, {})} | custom-call | flops 6710886400 | bytes 8388608 | tf_op jit(solution)/shard_map/pallas_call | solution.py:90
  410.2 0.2 collective-permute-start.5
  410.4 1.1 collective-permute-done.5
  411.5 1.2 collective-permute-start.6
  412.8 4.5 %collective-permute-done.6 = bf16[256,256]{1,0:T(8,128)(2,1)S(1)} collective-permute-done((bf16[256,256]{1,0:T(8,128)(2,1)S(1)}, bf16[256,256]{1,0:T(8,128)(2,1)S(1)}, u32[]{:S(2)}, u32[]{:S(2)}) %collective-permute-start.6) | collective-permute-done | bytes 131104 | tf_op jit(solution)/shard_map/ppermute | solution.py:120
  417.3 1.6 collective-permute-start.7
  418.9 3.5 collective-permute-done.7
  422.4 2.5 collective-permute-start.8
  424.9 5.0 %collective-permute-done.8 = bf16[256,256]{1,0:T(8,128)(2,1)S(1)} collective-permute-done((bf16[256,256]{1,0:T(8,128)(2,1)S(1)}, bf16[256,256]{1,0:T(8,128)(2,1)S(1)}, u32[]{:S(2)}, u32[]{:S(2)}) %collective-permute-start.8) | collective-permute-done | bytes 131104 | tf_op jit(solution)/shard_map/ppermute | solution.py:120
  429.9 0.0 copy-done.6
  429.9 0.9 pad_maximum_fusion.7
  (7 shorter events, 0.2 us)
Async XLA Ops:
  7.2 175.6 %all-gather.5.cloned.1.call-start = ((), (), s32[]{:S(2)}) async-start(), calls=%async_computation.1 | async-start | bytes 35651584 | tf_op jit(solution)/shard_map/all_gather | solution.py:144
  11.8 346.2 %all-gather.3.cloned.1.call-start = ((), (), s32[]{:S(2)}) async-start(), calls=%async_computation | async-start | bytes 35651584 | tf_op jit(solution)/shard_map/all_gather | solution.py:144
  12.6 93.9 %collective-permute-start = (bf16[256,8192]{1,0:T(8,128)(2,1)}, bf16[256,8192]{1,0:T(8,128)(2,1)}, u32[]{:S(2)}, u32[]{:S(2)}) collective-permute-start(bf16[256,8192]{1,0:T(8,128)(2,1)} %param.7), channel_id=1, source_target_pairs={{0,1},{1,0},{2,3},{3,2},{4,5},{5,4},{6,7},{7,6},{8,9},{9,8},{10,11... | collective-permute-start | bytes 12582920 | tf_op jit(solution)/shard_map/ppermute | solution.py:131
  182.7 24.0 %copy-start.2 = (bf16[512,512]{1,0:T(8,128)(2,1)S(1)}, bf16[512,512]{1,0:T(8,128)(2,1)}, u32[]{:S(2)}) copy-start(bf16[512,512]{1,0:T(8,128)(2,1)} %k_ref.3) | copy-start | bytes 1572868
  182.7 24.1 %copy-start.3 = (bf16[512,512]{1,0:T(8,128)(2,1)S(1)}, bf16[512,512]{1,0:T(8,128)(2,1)}, u32[]{:S(2)}) copy-start(bf16[512,512]{1,0:T(8,128)(2,1)} %v_ref.3) | copy-start | bytes 1572868
  182.7 24.1 %copy-start.4 = (bf16[128,512]{1,0:T(8,128)(2,1)S(1)}, bf16[128,512]{1,0:T(8,128)(2,1)}, u32[]{:S(2)}) copy-start(bf16[128,512]{1,0:T(8,128)(2,1)} %pk_ref.3) | copy-start | bytes 393220
  182.7 24.1 %copy-start.5 = (bf16[128,512]{1,0:T(8,128)(2,1)S(1)}, bf16[128,512]{1,0:T(8,128)(2,1)}, u32[]{:S(2)}) copy-start(bf16[128,512]{1,0:T(8,128)(2,1)} %pv_ref.3) | copy-start | bytes 393220
  206.8 2.2 copy-start
  235.0 1.3 collective-permute-start.1
  236.4 9.0 %collective-permute-start.2 = (bf16[256,256]{1,0:T(8,128)(2,1)S(1)}, bf16[256,256]{1,0:T(8,128)(2,1)S(1)}, u32[]{:S(2)}, u32[]{:S(2)}) collective-permute-start(bf16[256,256]{1,0:T(8,128)(2,1)S(1)} %add_convert_fusion.5), channel_id=1, source_target_pairs={{0,4},{2,6},{4,0},{6,2},{8,12},{10,14},{12,8},{14,10},{16,20},{18,... | collective-permute-start | bytes 393224 | tf_op jit(solution)/shard_map/ppermute | solution.py:120
  245.4 8.7 %collective-permute-start.3 = (bf16[256,256]{1,0:T(8,128)(2,1)S(1)}, bf16[256,256]{1,0:T(8,128)(2,1)S(1)}, u32[]{:S(2)}, u32[]{:S(2)}) collective-permute-start(bf16[256,256]{1,0:T(8,128)(2,1)S(1)} %add_convert_fusion.4), channel_id=1, source_target_pairs={{0,8},{2,10},{4,12},{6,14},{8,0},{10,2},{12,4},{14,6},{16,24},{18,... | collective-permute-start | bytes 393224 | tf_op jit(solution)/shard_map/ppermute | solution.py:120
  254.1 11.8 %collective-permute-start.4 = (bf16[256,256]{1,0:T(8,128)(2,1)S(1)}, bf16[256,256]{1,0:T(8,128)(2,1)S(1)}, u32[]{:S(2)}, u32[]{:S(2)}) collective-permute-start(bf16[256,256]{1,0:T(8,128)(2,1)S(1)} %add_convert_fusion.3), channel_id=1, source_target_pairs={{0,16},{2,18},{4,20},{6,22},{8,24},{10,26},{12,28},{14,30},{16,0},... | collective-permute-start | bytes 393224 | tf_op jit(solution)/shard_map/ppermute | solution.py:120
  381.9 2.2 copy-start.1
  384.1 45.7 %copy-start.6 = (f32[256,256]{1,0:T(8,128)S(1)}, f32[256,256]{1,0:T(8,128)}, u32[]{:S(2)}) copy-start(f32[256,256]{1,0:T(8,128)} %convert_add_fusion.1) | copy-start | bytes 786436
  410.2 1.3 collective-permute-start.5
  411.5 5.7 %collective-permute-start.6 = (bf16[256,256]{1,0:T(8,128)(2,1)S(1)}, bf16[256,256]{1,0:T(8,128)(2,1)S(1)}, u32[]{:S(2)}, u32[]{:S(2)}) collective-permute-start(bf16[256,256]{1,0:T(8,128)(2,1)S(1)} %add_convert_fusion.2), channel_id=1, source_target_pairs={{0,4},{2,6},{4,0},{6,2},{8,12},{10,14},{12,8},{14,10},{16,20},{18,... | collective-permute-start | bytes 393224 | tf_op jit(solution)/shard_map/ppermute | solution.py:120
  417.3 5.0 %collective-permute-start.7 = (bf16[256,256]{1,0:T(8,128)(2,1)S(1)}, bf16[256,256]{1,0:T(8,128)(2,1)S(1)}, u32[]{:S(2)}, u32[]{:S(2)}) collective-permute-start(bf16[256,256]{1,0:T(8,128)(2,1)S(1)} %add_convert_fusion.1), channel_id=1, source_target_pairs={{0,8},{2,10},{4,12},{6,14},{8,0},{10,2},{12,4},{14,6},{16,24},{18,... | collective-permute-start | bytes 393224 | tf_op jit(solution)/shard_map/ppermute | solution.py:120
  422.4 7.5 %collective-permute-start.8 = (bf16[256,256]{1,0:T(8,128)(2,1)S(1)}, bf16[256,256]{1,0:T(8,128)(2,1)S(1)}, u32[]{:S(2)}, u32[]{:S(2)}) collective-permute-start(bf16[256,256]{1,0:T(8,128)(2,1)S(1)} %add_convert_fusion), channel_id=1, source_target_pairs={{0,16},{2,18},{4,20},{6,22},{8,24},{10,26},{12,28},{14,30},{16,0},... | collective-permute-start | bytes 393224 | tf_op jit(solution)/shard_map/ppermute | solution.py:120
Sparse Core Ops, SparseCore 0:
  11.9 170.7 all-gather.4
  184.3 173.6 all-gather.2
